TPU v7x, 512 devices: a whole 4x4x16 slice. The times are simulated.
512 devices in a mesh: dp: 64 (over z, x), tensor: 8 (over y, core).
Axes of the slice: x: 4, y: 4, z: 16, core: 2. Of those that a mesh axis runs over, the one named last changes fastest.
Arguments:
- grad_query: bfloat16 [64, 1024, 2048], P('dp', None, 'tensor'), may hold values from -6 to 6
- error_query: bfloat16 [64, 1024, 2048], P('dp', None, 'tensor'), may hold values from -4 to 4
- basis_query: float32 [2048, 32], P('tensor'), may hold values from -6 to 6
- grad_output: bfloat16 [64, 2048, 1024], P('dp', 'tensor'), may hold values from -6 to 6
- error_output: bfloat16 [64, 2048, 1024], P('dp', 'tensor'), may hold values from -4 to 4
- basis_output: float32 [1024, 32], replicated, may hold values from -6 to 6
Outputs:
- reduced_query: bfloat16 [1024, 2048], P(None, 'tensor')
- reduced_output: bfloat16 [2048, 1024], P('tensor')
- error_query_next: bfloat16 [64, 1024, 2048], P('dp', None, 'tensor')
- error_output_next: bfloat16 [64, 2048, 1024], P('dp', 'tensor')
- basis_query_next: float32 [2048, 32], P('tensor')
- basis_output_next: float32 [1024, 32], replicated
All inputs are finite; a program needn't handle non-finite values.
Results may differ from a plain program's by a relative error of at most 0.001.
Values sent between devices are 32-bit elements; how exact they have to be, the bound alone decides.
A program may use at most 64 MiB of HBM per device.

v0:
```python
import jax
import jax.numpy as jnp
from jax import lax
from jax.sharding import PartitionSpec as P


def product(left, right):
    return jnp.dot(left, right, precision=lax.Precision.HIGHEST, preferred_element_type=jnp.float32)


def solve_lower(gram_matrix, factor):
    lower_factor = jnp.linalg.cholesky(gram_matrix)
    return lax.linalg.triangular_solve(
        lower_factor, factor, left_side=False, lower=True, transpose_a=True
    )


def local(grad_query, error_query, basis_query, grad_output, error_output, basis_output):
    replicas = lax.axis_size("dp")
    merged_query = grad_query[0].astype(jnp.float32) + error_query[0].astype(jnp.float32)
    merged_output = grad_output[0].astype(jnp.float32) + error_output[0].astype(jnp.float32)
    partial_query = product(merged_query, basis_query)
    partial_output = product(merged_output, basis_output)
    left_output = lax.psum(partial_output, "dp")
    left_query = lax.psum(partial_query, ("dp", "tensor"))
    unit_query = solve_lower(product(left_query.T, left_query), left_query)
    output_gram = lax.psum(product(left_output.T, left_output), "tensor")
    unit_output = solve_lower(output_gram, left_output)
    coeff_query = product(merged_query.T, unit_query)
    coeff_output = product(merged_output.T, unit_output)
    right_query = lax.psum(coeff_query, "dp")
    right_output = lax.psum(coeff_output, ("dp", "tensor"))
    approx_query = product(unit_query, right_query.T)
    approx_output = product(unit_output, right_output.T)
    error_query_next = (merged_query - approx_query / replicas).astype(jnp.bfloat16)[None]
    error_output_next = (merged_output - approx_output / replicas).astype(jnp.bfloat16)[None]
    return (
        approx_query.astype(jnp.bfloat16),
        approx_output.astype(jnp.bfloat16),
        error_query_next,
        error_output_next,
        right_query,
        right_output,
    )


def solution(mesh):
    return jax.shard_map(
        local,
        mesh=mesh,
        in_specs=(
            P("dp", None, "tensor"),
            P("dp", None, "tensor"),
            P("tensor", None),
            P("dp", "tensor", None),
            P("dp", "tensor", None),
            P(),
        ),
        out_specs=(
            P(None, "tensor"),
            P("tensor", None),
            P("dp", None, "tensor"),
            P("dp", "tensor", None),
            P("tensor", None),
            P(),
        ),
        check_vma=False,
    )
```

profile of v0, /device:TPU:8, one launch (start us, length us, event | category | flops | bytes accessed | tf_op | source)
XLA Modules:
  0.0 1075.3 jit_solution(7830386218565516968)
XLA Ops:
  7.2 0.0 copy-start
  7.2 0.0 copy-start.3
  7.2 0.0 copy-start.4
  7.2 0.0 all-reduce.3.cloned.1.call-start
  7.2 0.8 copy-done
  8.1 2.2 fusion.2
  10.3 285.6 %psum.37 = f32[256,32]{0,1:T(8,128)S(1)} all-reduce(f32[256,32]{0,1:T(8,128)S(1)} %fusion.2), channel_id=1, replica_groups=mesh['dp'=64,'tensor'=8] {'dp'}, use_global_device_ids=true, to_apply=%region_4.0 | all-reduce | flops 8192 | bytes 65536 | tf_op jit(solution)/shard_map/psum | solution.py:24
  295.9 0.2 fusion.21
  296.1 20.6 %psum.38 = f32[32,32]{0,1:T(8,128)S(1)} all-reduce(f32[32,32]{0,1:T(8,128)S(1)} %fusion.21), channel_id=1, replica_groups=mesh['dp'=64,'tensor'=8] {'tensor'}, use_global_device_ids=true, to_apply=%region_5.7 | all-reduce | flops 1024 | bytes 8192 | tf_op jit(solution)/shard_map/psum | solution.py:27
  316.7 0.1 copy.14
  316.8 2.9 cholesky.55
  319.7 0.6 compare_reduce_fusion
  320.4 0.7 fusion.13
  321.0 2.4 custom-call.9
  323.5 0.2 fusion.14
  323.7 0.0 copy-done.3
  323.7 0.0 copy-done.4
  323.8 0.0 copy-start.1
  323.8 0.0 copy-start.2
  323.8 0.0 copy-start.8
  323.8 1.5 fusion
  325.3 0.0 copy-done.1
  325.3 0.0 copy-done.2
  325.3 0.0 copy-done.8
  325.3 1.8 fusion.7
  327.1 0.0 all-reduce.3.cloned.1.call-update
  327.1 450.6 %all-reduce.3.cloned.1.call-done = (f32[1024,32]{0,1:T(8,128)}, f32[1024,32]{0,1:T(8,128)}) async-done(((f32[1024,32]{0,1:T(8,128)}, f32[1024,32]{0,1:T(8,128)}), (f32[1024,32]{0,1:T(8,128)}, f32[1024,32]{0,1:T(8,128)})) %all-reduce.3.cloned.1.call-update) | async-done | bytes 262160 | tf_op jit(solution)/shard_map/psum | solution.py:25
  777.7 1.2 fusion.20
  778.9 0.0 copy-start.5
  778.9 0.1 copy.12
  779.0 2.9 cholesky.44
  782.0 0.6 compare_reduce_fusion.1
  782.6 0.7 fusion.12
  783.3 2.4 custom-call.8
  785.7 0.0 copy-done.5
  785.7 0.3 fusion.17
  786.0 0.8 fusion.5
  786.8 276.8 %psum.36 = f32[256,32]{0,1:T(8,128)S(1)} all-reduce(f32[256,32]{0,1:T(8,128)S(1)} %fusion.5), channel_id=1, replica_groups=mesh['dp'=64,'tensor'=8] {'dp'}, use_global_device_ids=true, to_apply=%region_3.0 | all-reduce | flops 8192 | bytes 65536 | tf_op jit(solution)/shard_map/psum | solution.py:31
  1063.6 0.0 copy-start.7
  1063.6 0.0 copy-start.6
  1063.6 2.1 fusion.10
  1065.7 0.0 copy-done.7
  1065.7 0.0 copy-done.6
  1065.7 2.1 fusion.11
  1067.8 0.7 copy.18
  (4 shorter events, 0.1 us)
Async XLA Ops:
  7.2 0.9 copy-start
  7.2 316.6 %copy-start.3 = (bf16[1,256,1024]{2,1,0:T(8,128)(2,1)S(1)}, bf16[1,256,1024]{2,1,0:T(8,128)(2,1)}, u32[]{:S(2)}) copy-start(bf16[1,256,1024]{2,1,0:T(8,128)(2,1)} %param.11) | copy-start | bytes 1572868
  7.2 316.6 %copy-start.4 = (bf16[1,256,1024]{2,1,0:T(8,128)(2,1)S(1)}, bf16[1,256,1024]{2,1,0:T(8,128)(2,1)}, u32[]{:S(2)}) copy-start(bf16[1,256,1024]{2,1,0:T(8,128)(2,1)} %param.10) | copy-start | bytes 1572868
  7.2 770.5 %all-reduce.3.cloned.1.call-start = ((), (), s32[]{:S(2)}) async-start(), calls=%async_computation | async-start | bytes 524288 | tf_op jit(solution)/shard_map/psum | solution.py:25
  323.8 1.5 copy-start.1
  323.8 1.5 copy-start.2
  323.8 1.5 copy-start.8
  778.9 6.8 copy-start.5
  1063.6 2.1 copy-start.7
  1063.6 2.1 copy-start.6
Sparse Core Ops, SparseCore 0:
  327.2 450.3 all-reduce.2
where the time goes:
time: 1080 us
  blocking collectives  583 us (54%)
  waiting for transfers between devices  451 us (42%)
  between operations  14.2 us (1%)
  other arithmetic  13.4 us (1%)
  matrix products  12.4 us (1%)
    psum x1, waiting for transfers between devices, local(): left_query = lax.psum(partial_query, ('dp', 'tensor'))  451 us
    psum x1, blocking collectives, local(): left_output = lax.psum(partial_output, 'dp')  286 us
    psum x1, blocking collectives, local(): right_query = lax.psum(coeff_query, 'dp')  277 us
  transfers between devices with their start and end apart: 1, of which 1 were waited for; matrix products, arithmetic and copies ran while one was open for 0% of the time, Pallas kernels for 0%

commit v1 on v0

v1 whole, which is shorter than its diff:
```python
import functools

import jax
import jax.numpy as jnp
from jax import lax
from jax.experimental import pallas as pl
from jax.experimental.pallas import tpu as pltpu
from jax.sharding import PartitionSpec as P

MESH = pl.DeviceIdType.MESH
F32 = jnp.float32
BF16 = jnp.bfloat16
R = 32
LANES = 128


def split3(a):
    high = a.astype(BF16)
    rest = a - high.astype(F32)
    middle = rest.astype(BF16)
    low = (rest - middle.astype(F32)).astype(BF16)
    return jnp.concatenate([high, middle, low], axis=0)


def fold3(p):
    return (p[2 * R :] + p[R : 2 * R]) + p[:R]


def rows_by_rows(a, m):
    return lax.dot_general(a, m, (((1,), (1,)), ((), ())), preferred_element_type=F32)


def rows_by_columns(a, m):
    return lax.dot_general(a, m, (((1,), (0,)), ((), ())), preferred_element_type=F32)


def exact(a, b, dims):
    return lax.dot_general(
        a, b, (dims, ((), ())), precision=lax.Precision.HIGHEST, preferred_element_type=F32
    )


def eliminate(work, first, last):
    row = lax.broadcasted_iota(jnp.int32, work.shape, 0)
    for j in range(first, last):
        pivot = work[j : j + 1, j : j + 1]
        inverse = lax.rsqrt(pivot)
        inverse = inverse * (1.5 - 0.5 * (pivot * inverse) * inverse)
        scaled = work[j : j + 1, :] * inverse
        column = work[:, j : j + 1] * inverse
        work = jnp.where(row > j, work - column * scaled, jnp.where(row == j, scaled, work))
    return work


def augmented(gram):
    rows = lax.broadcasted_iota(jnp.int32, (R, R), 0)
    columns = lax.broadcasted_iota(jnp.int32, (R, R), 1)
    eye = jnp.where(rows == columns, 1.0, 0.0).astype(F32)
    return jnp.concatenate([gram, eye], axis=1)


def exchange(
    nt, nx, na, nb,
    gq_hbm, eq_hbm, bq_hbm, go_hbm, eo_hbm, bo_hbm,
    uq_out, rq_out, uo_out, ro_out,
    gq, eq, bq, go, eo, bo, load_sem,
    sq, so, rq, ro, za, zb, agq, ago, gram_all,
    send_sem, recv_sem,
):
    dp = lax.axis_index("dp")
    t = lax.axis_index("tensor")
    z = dp // nx
    x = lax.rem(dp, nx)
    b = z // na
    a = lax.rem(z, na)

    def at(x_, a_, b_, t_):
        return ((b_ * na + a_) * nx + x_, t_)

    def turn(i, d, n):
        return lax.rem(i + d, n)

    plane = [(dt, dx) for dx in range(nx) for dt in range(nt) if dt or dx]

    barrier = pltpu.get_barrier_semaphore()
    for dt, dx in plane:
        pl.semaphore_signal(
            barrier, inc=1, device_id=at(turn(x, dx, nx), a, b, turn(t, dt, nt)), device_id_type=MESH
        )
    for d in range(1, na):
        pl.semaphore_signal(barrier, inc=1, device_id=at(x, turn(a, d, na), b, t), device_id_type=MESH)
    for d in range(1, nb):
        pl.semaphore_signal(barrier, inc=1, device_id=at(x, a, turn(b, d, nb), t), device_id_type=MESH)

    loads = []
    for i, (source, target) in enumerate(
        ((bq_hbm, bq), (gq_hbm, gq), (eq_hbm, eq), (bo_hbm, bo), (go_hbm, go), (eo_hbm, eo))
    ):
        copy = pltpu.make_async_copy(source, target, load_sem.at[i])
        copy.start()
        loads.append(copy)

    def remote(source, target, k, device):
        pltpu.make_async_remote_copy(
            src_ref=source, dst_ref=target, send_sem=send_sem.at[k], recv_sem=recv_sem.at[k],
            device_id=device, device_id_type=MESH,
        ).start()

    def arrived(ref, k):
        pltpu.make_async_copy(ref, ref, recv_sem.at[k]).wait()

    def sent(ref, k):
        pltpu.make_async_copy(ref, ref, send_sem.at[k]).wait()

    def scatter(p, wide, narrow):
        k = 8 * p
        part = R // nx
        for i in range(nt):
            for j in range(nx):
                sq[p, i, j] = wide[j * part : (j + 1) * part, i * LANES : (i + 1) * LANES]
        for j in range(nx):
            so[p, j] = narrow[j * part : (j + 1) * part]
        for dx in range(1, nx):
            there = turn(x, dx, nx)
            remote(so.at[p, there], ro.at[p, dx - 1], k + 1, at(there, a, b, t))
        for i, (dt, dx) in enumerate(plane):
            tt, xx = turn(t, dt, nt), turn(x, dx, nx)
            remote(sq.at[p, tt, xx], rq.at[p, i], k, at(xx, a, b, tt))

    def gathered_sum(p):
        k = 8 * p
        arrived(ro.at[p], k + 1)
        narrow = so[p, x]
        for d in range(nx - 1):
            narrow = narrow + ro[p, d]
        arrived(rq.at[p], k)
        terms = [sq[p, t, x]] + [rq[p, i] for i in range(len(plane))]
        while len(terms) > 1:
            terms = [sum(terms[i : i + 2][1:], terms[i]) for i in range(0, len(terms), 2)]
        za[p, a, :, :LANES] = terms[0]
        za[p, a, :, LANES:] = narrow
        for d in range(1, na):
            remote(za.at[p, a], za.at[p, a], k + 2, at(x, turn(a, d, na), b, t))

    def along_a(p):
        k = 8 * p
        arrived(za.at[p, pl.ds(0, na - 1)], k + 2)
        total = za[p, 0]
        for i in range(1, na):
            total = total + za[p, i]
        zb[p, b] = total
        for d in range(1, nb):
            remote(zb.at[p, b], zb.at[p, b], k + 3, at(x, a, turn(b, d, nb), t))

    def along_b(p):
        k = 8 * p
        arrived(zb.at[p, pl.ds(0, nb - 1)], k + 3)
        total = zb[p, 0]
        for i in range(1, nb):
            total = total + zb[p, i]
        here = t * nx + x
        agq[p, here] = total[:, :LANES]
        ago[p, x] = total[:, LANES:]
        for dx in range(1, nx):
            remote(ago.at[p, x], ago.at[p, x], k + 5, at(turn(x, dx, nx), a, b, t))
        for dt, dx in plane:
            remote(agq.at[p, here], agq.at[p, here], k + 4, at(turn(x, dx, nx), a, b, turn(t, dt, nt)))

    def narrow_result(p):
        arrived(ago.at[p, pl.ds(0, nx - 1)], 8 * p + 5)
        return jnp.concatenate([ago[p, j] for j in range(nx)], axis=0)

    def wide_result(p):
        arrived(agq.at[p, pl.ds(0, nt * nx - 1)], 8 * p + 4)
        return jnp.concatenate(
            [jnp.concatenate([agq[p, i * nx + j] for j in range(nx)], axis=0) for i in range(nt)], axis=1
        )

    for i in range(3):
        loads[i].wait()
    terms = split3(bq[...].T)
    wide = fold3(rows_by_rows(terms, gq[...]) + rows_by_rows(terms, eq[...]))
    for i in range(3, 6):
        loads[i].wait()
    terms = split3(bo[...].T)
    narrow = fold3(rows_by_rows(terms, go[...]) + rows_by_rows(terms, eo[...]))
    pl.semaphore_wait(barrier, len(plane) + na - 1 + nb - 1)
    scatter(0, wide, narrow)
    gathered_sum(0)
    along_a(0)
    along_b(0)
    left_output = narrow_result(0)
    terms = split3(left_output)
    wide = fold3(rows_by_columns(terms, go[...]) + rows_by_columns(terms, eo[...]))
    left_query = wide_result(0)
    terms = split3(left_query)
    narrow = fold3(rows_by_columns(terms, gq[...]) + rows_by_columns(terms, eq[...]))

    scatter(1, wide, narrow)
    gram = exact(left_output, left_output, ((1,), (1,)))
    gram_all[t] = jnp.concatenate([gram, jnp.zeros((R, LANES - R), F32)], axis=1)
    for d in range(1, nt):
        remote(gram_all.at[t], gram_all.at[t], 6, at(x, a, b, turn(t, d, nt)))
    query_work = augmented(exact(left_query, left_query, ((1,), (1,))))
    gathered_sum(1)
    arrived(gram_all.at[pl.ds(0, nt - 1)], 6)
    gram = gram_all[0]
    for i in range(1, nt):
        gram = gram + gram_all[i]
    output_work = augmented(gram[:, :R])
    query_work = eliminate(query_work, 0, R // 2)
    output_work = eliminate(output_work, 0, R // 2)
    along_a(1)
    query_work = eliminate(query_work, R // 2, R)
    output_work = eliminate(output_work, R // 2, R)
    query_inverse = query_work[:, R : 2 * R]
    output_inverse = output_work[:, R : 2 * R]
    along_b(1)
    uq_out[...] = exact(query_inverse, left_query, ((1,), (0,)))
    uo_out[...] = exact(output_inverse, left_output, ((1,), (0,)))
    rq_out[...] = exact(query_inverse, narrow_result(1), ((1,), (0,)))
    ro_out[...] = exact(output_inverse, wide_result(1), ((1,), (0,)))

    for p in range(2):
        k = 8 * p
        sent(rq.at[p], k)
        sent(ro.at[p], k + 1)
        sent(za.at[p, pl.ds(0, na - 1)], k + 2)
        sent(zb.at[p, pl.ds(0, nb - 1)], k + 3)
        sent(agq.at[p, pl.ds(0, nt * nx - 1)], k + 4)
        sent(ago.at[p, pl.ds(0, nx - 1)], k + 5)
    sent(gram_all.at[pl.ds(0, nt - 1)], 6)


def stacked(left, right):
    left_high = left.astype(BF16)
    left_low = (left - left_high.astype(F32)).astype(BF16)
    right_high = right.astype(BF16)
    right_low = (right - right_high.astype(F32)).astype(BF16)
    return lax.dot_general(
        jnp.concatenate([left_high, left_low, left_high], axis=0),
        jnp.concatenate([right_high, right_high, right_low], axis=0),
        (((0,), (0,)), ((), ())),
        preferred_element_type=F32,
    )


def finish(
    replicas, uq, rq, uo, ro, gq, eq, go, eo,
    reduced_query, reduced_output, error_query, error_output, right_query, right_output,
):
    scale = 1.0 / replicas
    approx = stacked(uq[...], rq[...])
    reduced_query[...] = approx.astype(BF16)
    error_query[...] = (gq[...].astype(F32) + eq[...].astype(F32) - approx * scale).astype(BF16)
    approx = stacked(uo[...], ro[...])
    reduced_output[...] = approx.astype(BF16)
    error_output[...] = (go[...].astype(F32) + eo[...].astype(F32) - approx * scale).astype(BF16)
    right_query[...] = rq[...].T
    right_output[...] = ro[...].T


def local(sizes, grad_query, error_query, basis_query, grad_output, error_output, basis_output):
    nt, nx, na, nb = sizes
    gq, eq, go, eo = grad_query[0], error_query[0], grad_output[0], error_output[0]
    rows, columns = gq.shape
    hidden, features = go.shape
    part = R // nx
    any_space = pl.BlockSpec(memory_space=pl.ANY)
    vmem = pl.BlockSpec(memory_space=pltpu.VMEM)
    shape = jax.ShapeDtypeStruct
    uq, rq, uo, ro = pl.pallas_call(
        functools.partial(exchange, nt, nx, na, nb),
        out_shape=(
            shape((R, rows), F32), shape((R, columns), F32), shape((R, hidden), F32), shape((R, features), F32),
        ),
        in_specs=[any_space] * 6,
        out_specs=(vmem,) * 4,
        scratch_shapes=[
            pltpu.VMEM((rows, columns), BF16),
            pltpu.VMEM((rows, columns), BF16),
            pltpu.VMEM((columns, R), F32),
            pltpu.VMEM((hidden, features), BF16),
            pltpu.VMEM((hidden, features), BF16),
            pltpu.VMEM((features, R), F32),
            pltpu.SemaphoreType.DMA((6,)),
            pltpu.VMEM((2, nt, nx, part, LANES), F32),
            pltpu.VMEM((2, nx, part, hidden), F32),
            pltpu.VMEM((2, nt * nx - 1, part, LANES), F32),
            pltpu.VMEM((2, nx - 1, part, hidden), F32),
            pltpu.VMEM((2, na, part, LANES + hidden), F32),
            pltpu.VMEM((2, nb, part, LANES + hidden), F32),
            pltpu.VMEM((2, nt * nx, part, LANES), F32),
            pltpu.VMEM((2, nx, part, hidden), F32),
            pltpu.VMEM((nt, R, LANES), F32),
            pltpu.SemaphoreType.DMA((16,)),
            pltpu.SemaphoreType.DMA((16,)),
        ],
        compiler_params=pltpu.CompilerParams(
            collective_id=0, has_side_effects=True, vmem_limit_bytes=32 * 1024 * 1024
        ),
    )(gq, eq, basis_query, go, eo, basis_output)
    outs = pl.pallas_call(
        functools.partial(finish, nx * na * nb),
        out_shape=(
            shape((rows, columns), BF16), shape((hidden, features), BF16),
            shape((rows, columns), BF16), shape((hidden, features), BF16),
            shape((columns, R), F32), shape((features, R), F32),
        ),
        in_specs=[vmem] * 8,
        out_specs=(vmem,) * 6,
        compiler_params=pltpu.CompilerParams(vmem_limit_bytes=32 * 1024 * 1024),
    )(uq, rq, uo, ro, gq, eq, go, eo)
    return outs[0], outs[1], outs[2][None], outs[3][None], outs[4], outs[5]


def solution(mesh):
    nt, n = mesh.shape["tensor"], mesh.shape["dp"]
    nx = 4 if n >= 64 else 2
    na = 4 if n >= 64 else 2
    nb = n // (nx * na)
    return jax.shard_map(
        functools.partial(local, (nt, nx, na, nb)),
        mesh=mesh,
        in_specs=(
            P("dp", None, "tensor"),
            P("dp", None, "tensor"),
            P("tensor", None),
            P("dp", "tensor", None),
            P("dp", "tensor", None),
            P(),
        ),
        out_specs=(
            P(None, "tensor"),
            P("tensor", None),
            P("dp", None, "tensor"),
            P("dp", "tensor", None),
            P("tensor", None),
            P(),
        ),
        check_vma=False,
    )
```

time: 1080 us -> 72.1 us (0.07)
  the two profiles are of different devices: /device:TPU:8 before, /device:TPU:1 now
where the time goes in v1:
time: 72.1 us; the launch traced here: 71.8 us
  Pallas kernels  65.4 us (91%)
  local copies, waits for them, and re-layouts  5.76 us (8%)
    pallas_call x1, Pallas kernels, local(): pl.pallas_call(functools.partial(exchange, nt, nx, na, nb), out_shape=(sh...  63.5 us
    unnamed x14, local copies, waits for them, and re-layouts  5.76 us
    pallas_call x1, Pallas kernels, local(): pl.pallas_call(functools.partial(finish, nx * na * nb), out_shape=(shape(...  1.87 us

profile of v1, /device:TPU:1, one launch (start us, length us, event | category | flops | bytes accessed | tf_op | source)
XLA Modules:
  0.0 71.8 jit_solution(6104598481970497519)
XLA Ops:
  0.6 0.0 copy-start.4
  0.6 0.0 copy-start
  0.7 0.9 %copy.12.bq_hbm = f32[256,32]{1,0:T(8,128)S(1)} copy(f32[256,32]{0,1:T(8,128)} %param.8) | data formatting | bytes 65536 | tf_op args[2]
  1.6 0.0 copy-done.4
  1.6 0.2 copy.13.bo_hbm
  1.8 0.0 copy-done
  1.8 0.0 copy-start.1
  1.8 1.0 %copy-done.1 = bf16[1,1024,256]{2,1,0:T(8,128)(2,1)S(1)} copy-done((bf16[1,1024,256]{2,1,0:T(8,128)(2,1)S(1)}, bf16[1,1024,256]{2,1,0:T(8,128)(2,1)}, u32[]{:S(2)}) %copy-start.1) | copy-done | bytes 524312
  2.8 0.0 copy-start.2
  2.8 1.0 %copy-done.2 = bf16[1,256,1024]{2,1,0:T(8,128)(2,1)S(1)} copy-done((bf16[1,256,1024]{2,1,0:T(8,128)(2,1)S(1)}, bf16[1,256,1024]{2,1,0:T(8,128)(2,1)}, u32[]{:S(2)}) %copy-start.2) | copy-done | bytes 524312
  3.9 0.0 copy-start.3
  3.9 1.0 %copy-done.3 = bf16[1,256,1024]{2,1,0:T(8,128)(2,1)S(1)} copy-done((bf16[1,256,1024]{2,1,0:T(8,128)(2,1)S(1)}, bf16[1,256,1024]{2,1,0:T(8,128)(2,1)}, u32[]{:S(2)}) %copy-start.3) | copy-done | bytes 524312
  4.9 63.5 %shard_map.109 = (f32[32,1024]{1,0:T(8,128)S(1)}, f32[32,256]{1,0:T(8,128)S(1)}, f32[32,256]{1,0:T(8,128)S(1)}, f32[32,1024]{1,0:T(8,128)S(1)}) custom-call(bf16[1024,256]{1,0:T(8,128)(2,1)S(1)} %bitcast.6, bf16[1024,256]{1,0:T(8,128)(2,1)S(1)} %bitcast.8, f32[256,32]{1,0:T(8,128)S(1)} %copy.12.bq_hbm, bf16[256,1024]{1,0:T(8,128)(2,1)S(1)} %bitcast.10, ...), custom_call_target="tpu_custom_call" | custom-call | tf_op jit(solution)/shard_map/pallas_call | solution.py:272
  68.4 1.9 %shard_map.110 = (bf16[1024,256]{1,0:T(8,128)(2,1)}, bf16[256,1024]{1,0:T(8,128)(2,1)}, bf16[1024,256]{1,0:T(8,128)(2,1)}, bf16[256,1024]{1,0:T(8,128)(2,1)}, f3...) custom-call(f32[32,1024]{1,0:T(8,128)S(1)} %get-tuple-element.16.uq, f32[32,256]{1,0:T(8,128)S(1)} %get-tuple-element.17.rq, ...), custom_call_target="tpu_custom_call" | custom-call | tf_op jit(solution)/shard_map/pallas_call | solution.py:303
  70.3 0.7 copy.14
  71.0 0.8 %copy.15 = f32[1024,32]{0,1:T(8,128)} copy(f32[1024,32]{1,0:T(8,128)S(1)} %get-tuple-element.31) | data formatting | bytes 262144
Async XLA Ops:
  0.6 0.9 %copy-start.4 = (f32[1024,32]{0,1:T(8,128)S(1)}, f32[1024,32]{0,1:T(8,128)}, u32[]{:S(2)}) copy-start(f32[1024,32]{0,1:T(8,128)} %param.11) | copy-start | bytes 393220
  0.6 1.1 %copy-start = (bf16[1,1024,256]{2,1,0:T(8,128)(2,1)S(1)}, bf16[1,1024,256]{2,1,0:T(8,128)(2,1)}, u32[]{:S(2)}) copy-start(bf16[1,1024,256]{2,1,0:T(8,128)(2,1)} %param.6) | copy-start | bytes 1572868
  1.8 1.0 %copy-start.1 = (bf16[1,1024,256]{2,1,0:T(8,128)(2,1)S(1)}, bf16[1,1024,256]{2,1,0:T(8,128)(2,1)}, u32[]{:S(2)}) copy-start(bf16[1,1024,256]{2,1,0:T(8,128)(2,1)} %param.7) | copy-start | bytes 1572868
  2.8 1.0 %copy-start.2 = (bf16[1,256,1024]{2,1,0:T(8,128)(2,1)S(1)}, bf16[1,256,1024]{2,1,0:T(8,128)(2,1)}, u32[]{:S(2)}) copy-start(bf16[1,256,1024]{2,1,0:T(8,128)(2,1)} %param.9) | copy-start | bytes 1572868
  3.9 1.0 %copy-start.3 = (bf16[1,256,1024]{2,1,0:T(8,128)(2,1)S(1)}, bf16[1,256,1024]{2,1,0:T(8,128)(2,1)}, u32[]{:S(2)}) copy-start(bf16[1,256,1024]{2,1,0:T(8,128)(2,1)} %param.10) | copy-start | bytes 1572868

commit v2 on v1

v2 whole, which is shorter than its diff:
```python
import functools

import jax
import jax.numpy as jnp
from jax import lax
from jax.experimental import pallas as pl
from jax.experimental.pallas import tpu as pltpu
from jax.sharding import PartitionSpec as P

MESH = pl.DeviceIdType.MESH
F32 = jnp.float32
BF16 = jnp.bfloat16
R = 32
LANES = 128


def split3(a):
    high = a.astype(BF16)
    rest = a - high.astype(F32)
    middle = rest.astype(BF16)
    low = (rest - middle.astype(F32)).astype(BF16)
    return jnp.concatenate([high, middle, low], axis=0)


def fold3(p):
    return (p[2 * R :] + p[R : 2 * R]) + p[:R]


def rows_by_rows(a, m):
    return lax.dot_general(a, m, (((1,), (1,)), ((), ())), preferred_element_type=F32)


def rows_by_columns(a, m):
    return lax.dot_general(a, m, (((1,), (0,)), ((), ())), preferred_element_type=F32)


def exact(a, b, dims):
    return lax.dot_general(
        a, b, (dims, ((), ())), precision=lax.Precision.HIGHEST, preferred_element_type=F32
    )


def eliminate(work, first, last):
    row = lax.broadcasted_iota(jnp.int32, work.shape, 0)
    for j in range(first, last):
        pivot = work[j : j + 1, j : j + 1]
        inverse = lax.rsqrt(pivot)
        inverse = inverse * (1.5 - 0.5 * (pivot * inverse) * inverse)
        scaled = work[j : j + 1, :] * inverse
        column = work[:, j : j + 1] * inverse
        work = jnp.where(row > j, work - column * scaled, jnp.where(row == j, scaled, work))
    return work


def augmented(gram):
    rows = lax.broadcasted_iota(jnp.int32, (R, R), 0)
    columns = lax.broadcasted_iota(jnp.int32, (R, R), 1)
    eye = jnp.where(rows == columns, 1.0, 0.0).astype(F32)
    return jnp.concatenate([gram, eye], axis=1)


def exchange(
    ny, nc, nx, na, nb,
    gq_hbm, eq_hbm, bq_hbm, go_hbm, eo_hbm, bo_hbm,
    uq_out, rq_out, uo_out, ro_out,
    gq, eq, bq, go, eo, bo, load_sem,
    wide_here, wide_in, wide_z, wide_all,
    thin_here, thin_in, thin_a, thin_b, thin_all,
    gram_all, send_sem, recv_sem,
):
    nt, nz = ny * nc, na * nb
    part = R // nx
    dp = lax.axis_index("dp")
    t = lax.axis_index("tensor")
    z = dp // nx
    x = lax.rem(dp, nx)
    b = z // na
    a = lax.rem(z, na)
    y = t // nc
    c = lax.rem(t, nc)

    def hops(d, n):
        return min(d, n - d)

    plane = sorted(
        ((dy, dc, dx) for dx in range(nx) for dy in range(ny) for dc in range(nc) if dx or dy or dc),
        key=lambda d: -hops(d[0], ny) - hops(d[2], nx),
    )
    along_z = sorted(range(1, nz), key=lambda d: -hops(d, nz))
    along_x = sorted(range(1, nx), key=lambda d: -hops(d, nx))

    def turned_t(dy, dc):
        return lax.rem(y + dy, ny) * nc + lax.rem(c + dc, nc)

    def turned_x(dx):
        return lax.rem(x + dx, nx)

    def in_plane(t_, x_):
        return (z * nx + x_, t_)

    def at_z(z_):
        return (z_ * nx + x, t)

    def signal(device):
        pl.semaphore_signal(barrier, inc=1, device_id=device, device_id_type=MESH)

    barrier = pltpu.get_barrier_semaphore()
    for d in along_z:
        signal(at_z(lax.rem(z + d, nz)))
    for dy, dc, dx in plane:
        signal(in_plane(turned_t(dy, dc), turned_x(dx)))

    loads = []
    for i, (source, target) in enumerate(
        ((bo_hbm, bo), (go_hbm, go), (eo_hbm, eo), (bq_hbm, bq), (gq_hbm, gq), (eq_hbm, eq))
    ):
        copy = pltpu.make_async_copy(source, target, load_sem.at[i])
        copy.start()
        loads.append(copy)

    def remote(source, target, k, device):
        pltpu.make_async_remote_copy(
            src_ref=source, dst_ref=target, send_sem=send_sem.at[k], recv_sem=recv_sem.at[k],
            device_id=device, device_id_type=MESH,
        ).start()

    def arrived(ref, k):
        pltpu.make_async_copy(ref, ref, recv_sem.at[k]).wait()

    def sent(ref, k):
        pltpu.make_async_copy(ref, ref, send_sem.at[k]).wait()

    def total(terms):
        while len(terms) > 1:
            pairs = [terms[i] + terms[i + 1] for i in range(0, len(terms) - 1, 2)]
            terms = pairs + terms[len(pairs) * 2 :]
        return terms[0]

    def wide_scatter(p, value):
        for i in range(nt):
            for j in range(nx):
                wide_here[p, i, j] = value[j * part : (j + 1) * part, i * LANES : (i + 1) * LANES]
        for i, (dy, dc, dx) in enumerate(plane):
            t_, x_ = turned_t(dy, dc), turned_x(dx)
            remote(wide_here.at[p, t_, x_], wide_in.at[p, i], 8 * p, in_plane(t_, x_))

    def wide_exchange(p):
        arrived(wide_in.at[p], 8 * p)
        wide_z[p, z] = total([wide_here[p, t, x]] + [wide_in[p, i] for i in range(len(plane))])
        for d in along_z:
            remote(wide_z.at[p, z], wide_z.at[p, z], 8 * p + 1, at_z(lax.rem(z + d, nz)))

    def wide_gather(p):
        arrived(wide_z.at[p, pl.ds(0, nz - 1)], 8 * p + 1)
        here = t * nx + x
        wide_all[p, here] = total([wide_z[p, i] for i in range(nz)])
        for dy, dc, dx in plane:
            remote(
                wide_all.at[p, here], wide_all.at[p, here], 8 * p + 2, in_plane(turned_t(dy, dc), turned_x(dx))
            )

    def wide_result(p):
        arrived(wide_all.at[p, pl.ds(0, nt * nx - 1)], 8 * p + 2)
        return jnp.concatenate(
            [jnp.concatenate([wide_all[p, i * nx + j] for j in range(nx)], axis=0) for i in range(nt)], axis=1
        )

    def thin_scatter(p, value):
        for j in range(nx):
            thin_here[p, j] = value[j * part : (j + 1) * part]
        for i, dx in enumerate(along_x):
            x_ = turned_x(dx)
            remote(thin_here.at[p, x_], thin_in.at[p, i], 8 * p + 3, in_plane(t, x_))

    def thin_near(p):
        arrived(thin_in.at[p], 8 * p + 3)
        thin_a[p, a] = total([thin_here[p, x]] + [thin_in[p, i] for i in range(nx - 1)])
        for d in range(1, na):
            remote(thin_a.at[p, a], thin_a.at[p, a], 8 * p + 4, at_z(b * na + lax.rem(a + d, na)))

    def thin_far(p):
        arrived(thin_a.at[p, pl.ds(0, na - 1)], 8 * p + 4)
        thin_b[p, b] = total([thin_a[p, i] for i in range(na)])
        for d in range(1, nb):
            remote(thin_b.at[p, b], thin_b.at[p, b], 8 * p + 5, at_z(lax.rem(b + d, nb) * na + a))

    def thin_gather(p):
        arrived(thin_b.at[p, pl.ds(0, nb - 1)], 8 * p + 5)
        thin_all[p, x] = total([thin_b[p, i] for i in range(nb)])
        for dx in along_x:
            remote(thin_all.at[p, x], thin_all.at[p, x], 8 * p + 6, in_plane(t, turned_x(dx)))

    def thin_result(p):
        arrived(thin_all.at[p, pl.ds(0, nx - 1)], 8 * p + 6)
        return jnp.concatenate([thin_all[p, j] for j in range(nx)], axis=0)

    for i in range(3):
        loads[i].wait()
    terms = split3(bo[...])
    value = fold3(rows_by_rows(terms, go[...]) + rows_by_rows(terms, eo[...]))
    pl.semaphore_wait(barrier, len(plane) + len(along_z))
    thin_scatter(0, value)
    for i in range(3, 6):
        loads[i].wait()
    terms = split3(bq[...])
    value = fold3(rows_by_rows(terms, gq[...]) + rows_by_rows(terms, eq[...]))
    wide_scatter(0, value)
    thin_near(0)
    wide_exchange(0)
    thin_far(0)
    thin_gather(0)
    wide_gather(0)

    left_output = thin_result(0)
    terms = split3(left_output)
    value = fold3(rows_by_columns(terms, go[...]) + rows_by_columns(terms, eo[...]))
    wide_scatter(1, value)
    gram = exact(left_output, left_output, ((1,), (1,)))
    gram_all[t] = jnp.concatenate([gram[i : i + 8] for i in range(0, R, 8)], axis=1)
    for dy, dc, dx in plane:
        if dx == 0:
            remote(gram_all.at[t], gram_all.at[t], 7, in_plane(turned_t(dy, dc), x))
    left_query = wide_result(0)
    terms = split3(left_query)
    value = fold3(rows_by_columns(terms, gq[...]) + rows_by_columns(terms, eq[...]))
    thin_scatter(1, value)
    query_work = augmented(exact(left_query, left_query, ((1,), (1,))))
    wide_exchange(1)
    thin_near(1)
    arrived(gram_all.at[pl.ds(0, nt - 1)], 7)
    gram = total([gram_all[i] for i in range(nt)])
    gram = jnp.concatenate([gram[:, i : i + R] for i in range(0, 4 * R, R)], axis=0)
    output_work = augmented(gram)
    query_work = eliminate(query_work, 0, R // 2)
    output_work = eliminate(output_work, 0, R // 2)
    thin_far(1)
    query_work = eliminate(query_work, R // 2, R)
    output_work = eliminate(output_work, R // 2, R)
    query_inverse = query_work[:, R : 2 * R]
    output_inverse = output_work[:, R : 2 * R]
    uq_out[...] = exact(query_inverse, left_query, ((1,), (0,)))
    uo_out[...] = exact(output_inverse, left_output, ((1,), (0,)))
    wide_gather(1)
    thin_gather(1)
    ro_out[...] = exact(output_inverse, wide_result(1), ((1,), (0,)))
    rq_out[...] = exact(query_inverse, thin_result(1), ((1,), (0,)))

    for p in range(2):
        k = 8 * p
        sent(wide_in.at[p], k)
        sent(wide_z.at[p, pl.ds(0, nz - 1)], k + 1)
        sent(wide_all.at[p, pl.ds(0, nt * nx - 1)], k + 2)
        sent(thin_in.at[p], k + 3)
        sent(thin_a.at[p, pl.ds(0, na - 1)], k + 4)
        sent(thin_b.at[p, pl.ds(0, nb - 1)], k + 5)
        sent(thin_all.at[p, pl.ds(0, nx - 1)], k + 6)
    sent(gram_all.at[pl.ds(0, nt - 1)], 7)


def stacked(left, right):
    left_high = left.astype(BF16)
    left_low = (left - left_high.astype(F32)).astype(BF16)
    right_high = right.astype(BF16)
    right_low = (right - right_high.astype(F32)).astype(BF16)
    return lax.dot_general(
        jnp.concatenate([left_high, left_low, left_high], axis=0),
        jnp.concatenate([right_high, right_high, right_low], axis=0),
        (((0,), (0,)), ((), ())),
        preferred_element_type=F32,
    )


def finish(
    replicas, uq, rq, uo, ro, gq, eq, go, eo,
    reduced_query, reduced_output, error_query, error_output, right_query, right_output,
):
    scale = 1.0 / replicas
    approx = stacked(uq[...], rq[...])
    reduced_query[...] = approx.astype(BF16)
    error_query[...] = (gq[...].astype(F32) + eq[...].astype(F32) - approx * scale).astype(BF16)
    approx = stacked(uo[...], ro[...])
    reduced_output[...] = approx.astype(BF16)
    error_output[...] = (go[...].astype(F32) + eo[...].astype(F32) - approx * scale).astype(BF16)
    right_query[...] = rq[...]
    right_output[...] = ro[...]


def local(sizes, grad_query, error_query, basis_query, grad_output, error_output, basis_output):
    ny, nc, nx, na, nb = sizes
    nt = ny * nc
    gq, eq, go, eo = grad_query[0], error_query[0], grad_output[0], error_output[0]
    rows, columns = gq.shape
    hidden, features = go.shape
    part = R // nx
    hbm = pl.BlockSpec(memory_space=pltpu.HBM)
    vmem = pl.BlockSpec(memory_space=pltpu.VMEM)
    shape = jax.ShapeDtypeStruct
    uq, rq, uo, ro = pl.pallas_call(
        functools.partial(exchange, ny, nc, nx, na, nb),
        out_shape=(
            shape((R, rows), F32), shape((R, columns), F32), shape((R, hidden), F32), shape((R, features), F32),
        ),
        in_specs=[hbm] * 6,
        out_specs=(vmem,) * 4,
        scratch_shapes=[
            pltpu.VMEM((rows, columns), BF16),
            pltpu.VMEM((rows, columns), BF16),
            pltpu.VMEM((R, columns), F32),
            pltpu.VMEM((hidden, features), BF16),
            pltpu.VMEM((hidden, features), BF16),
            pltpu.VMEM((R, features), F32),
            pltpu.SemaphoreType.DMA((6,)),
            pltpu.VMEM((2, nt, nx, part, LANES), F32),
            pltpu.VMEM((2, nt * nx - 1, part, LANES), F32),
            pltpu.VMEM((2, na * nb, part, LANES), F32),
            pltpu.VMEM((2, nt * nx, part, LANES), F32),
            pltpu.VMEM((2, nx, part, hidden), F32),
            pltpu.VMEM((2, nx - 1, part, hidden), F32),
            pltpu.VMEM((2, na, part, hidden), F32),
            pltpu.VMEM((2, nb, part, hidden), F32),
            pltpu.VMEM((2, nx, part, hidden), F32),
            pltpu.VMEM((nt, 8, LANES), F32),
            pltpu.SemaphoreType.DMA((16,)),
            pltpu.SemaphoreType.DMA((16,)),
        ],
        compiler_params=pltpu.CompilerParams(
            collective_id=0, has_side_effects=True, vmem_limit_bytes=60 * 1024 * 1024
        ),
    )(gq, eq, basis_query.T, go, eo, basis_output.T)
    outs = pl.pallas_call(
        functools.partial(finish, nx * na * nb),
        out_shape=(
            shape((rows, columns), BF16), shape((hidden, features), BF16),
            shape((rows, columns), BF16), shape((hidden, features), BF16),
            shape((R, columns), F32), shape((R, features), F32),
        ),
        in_specs=[vmem] * 8,
        out_specs=(vmem,) * 6,
        compiler_params=pltpu.CompilerParams(vmem_limit_bytes=60 * 1024 * 1024),
    )(uq, rq, uo, ro, gq, eq, go, eo)
    return outs[0], outs[1], outs[2][None], outs[3][None], outs[4].T, outs[5].T


def solution(mesh):
    nt, n = mesh.shape["tensor"], mesh.shape["dp"]
    nx = 4 if n >= 64 else 2
    na = 4 if n >= 64 else 2
    nb = n // (nx * na)
    return jax.shard_map(
        functools.partial(local, (nt // 2, 2, nx, na, nb)),
        mesh=mesh,
        in_specs=(
            P("dp", None, "tensor"),
            P("dp", None, "tensor"),
            P("tensor", None),
            P("dp", "tensor", None),
            P("dp", "tensor", None),
            P(),
        ),
        out_specs=(
            P(None, "tensor"),
            P("tensor", None),
            P("dp", None, "tensor"),
            P("dp", "tensor", None),
            P("tensor", None),
            P(),
        ),
        check_vma=False,
    )
```

time: 72.1 us -> 62.8 us (0.87)
  the two profiles are of different devices: /device:TPU:1 before, /device:TPU:2 now
where the time goes in v2:
time: 62.8 us; the launch traced here: 62.6 us
  Pallas kernels  62 us (99%)
  between operations  0.64 us (1%)
    pallas_call x1, Pallas kernels, local(): pl.pallas_call(functools.partial(exchange, ny, nc, nx, na, nb), out_shape...  58.4 us
    pallas_call x1, Pallas kernels, local(): pl.pallas_call(functools.partial(finish, nx * na * nb), out_shape=(shape(...  3.53 us

profile of v2, /device:TPU:2, one launch (start us, length us, event | category | flops | bytes accessed | tf_op | source)
XLA Modules:
  0.0 62.6 jit_solution(13612263431567744395)
XLA Ops:
  0.6 58.4 %shard_map.109 = (f32[32,1024]{1,0:T(8,128)}, f32[32,256]{1,0:T(8,128)}, f32[32,256]{1,0:T(8,128)}, f32[32,1024]{1,0:T(8,128)}) custom-call(bf16[1024,256]{1,0:T(8,128)(2,1)} %bitcast.10, bf16[1024,256]{1,0:T(8,128)(2,1)} %bitcast.12, f32[32,256]{1,0:T(8,128)} %bitcast.19, bf16[256,1024]{1,0:T(8,128)(2,1)} %bitcast.14, bf16[256,1024]{1,0:T(8,128)(2,1)} %bitcast.16, ...), custom_call_target="tpu_custom_call" | custom-call | tf_op jit(solution)/shard_map/pallas_call | solution.py:298
  59.1 3.5 %shard_map.110 = (bf16[1024,256]{1,0:T(8,128)(2,1)}, bf16[256,1024]{1,0:T(8,128)(2,1)}, bf16[1024,256]{1,0:T(8,128)(2,1)}, bf16[256,1024]{1,0:T(8,128)(2,1)}, f32[32,256]{1,0:T(8,128)}, /*index=5*/f32[32,1024]{1,0:T(8,128)}) custom-call(f32[32,1024]{1,0:T(8,128)} %get-tuple-element.16.uq, f32[32,256]{1,0:T(8,128)} %get-tuple-element.17.rq, ...), custom_call_target="tpu_custom_call" | custom-call | tf_op jit(solution)/shard_map/pallas_call | solution.py:330

commit v3 on v2

--- a/solution.py
+++ b/solution.py
@@ -60,22 +60,20 @@
 
 
 def exchange(
-    ny, nc, nx, na, nb,
+    ny, nc, nx, nz,
     gq_hbm, eq_hbm, bq_hbm, go_hbm, eo_hbm, bo_hbm,
     uq_out, rq_out, uo_out, ro_out,
     gq, eq, bq, go, eo, bo, load_sem,
     wide_here, wide_in, wide_z, wide_all,
-    thin_here, thin_in, thin_a, thin_b, thin_all,
-    gram_all, send_sem, recv_sem,
+    thin_here, thin_in, thin_z, thin_zll,
+    gram_all, send_sem, recv_sem, relay_sem,
 ):
-    nt, nz = ny * nc, na * nb
+    nt = ny * nc
     part = R // nx
     dp = lax.axis_index("dp")
     t = lax.axis_index("tensor")
     z = dp // nx
     x = lax.rem(dp, nx)
-    b = z // na
-    a = lax.rem(z, na)
     y = t // nc
     c = lax.rem(t, nc)
 
@@ -87,6 +85,7 @@
         key=lambda d: -hops(d[0], ny) - hops(d[2], nx),
     )
     along_z = sorted(range(1, nz), key=lambda d: -hops(d, nz))
+    reach = nz // 4
     along_x = sorted(range(1, nx), key=lambda d: -hops(d, nx))
 
     def turned_t(dy, dc):
@@ -106,9 +105,8 @@
 
     barrier = pltpu.get_barrier_semaphore()
     for d in along_z:
-        signal(at_z(lax.rem(z + d, nz)))
-    for dy, dc, dx in plane:
-        signal(in_plane(turned_t(dy, dc), turned_x(dx)))
+        if hops(d, nz) <= reach:
+            signal(at_z(lax.rem(z + d, nz)))
 
     loads = []
     for i, (source, target) in enumerate(
@@ -117,6 +115,9 @@
         copy = pltpu.make_async_copy(source, target, load_sem.at[i])
         copy.start()
         loads.append(copy)
+
+    for dy, dc, dx in plane:
+        signal(in_plane(turned_t(dy, dc), turned_x(dx)))
 
     def remote(source, target, k, device):
         pltpu.make_async_remote_copy(
@@ -172,42 +173,38 @@
             x_ = turned_x(dx)
             remote(thin_here.at[p, x_], thin_in.at[p, i], 8 * p + 3, in_plane(t, x_))
 
-    def thin_near(p):
+    def thin_exchange(p):
         arrived(thin_in.at[p], 8 * p + 3)
-        thin_a[p, a] = total([thin_here[p, x]] + [thin_in[p, i] for i in range(nx - 1)])
-        for d in range(1, na):
-            remote(thin_a.at[p, a], thin_a.at[p, a], 8 * p + 4, at_z(b * na + lax.rem(a + d, na)))
-
-    def thin_far(p):
-        arrived(thin_a.at[p, pl.ds(0, na - 1)], 8 * p + 4)
-        thin_b[p, b] = total([thin_a[p, i] for i in range(na)])
-        for d in range(1, nb):
-            remote(thin_b.at[p, b], thin_b.at[p, b], 8 * p + 5, at_z(lax.rem(b + d, nb) * na + a))
+        thin_z[p, z] = total([thin_here[p, x]] + [thin_in[p, i] for i in range(nx - 1)])
+        for d in along_z:
+            remote(thin_z.at[p, z], thin_z.at[p, z], 8 * p + 4, at_z(lax.rem(z + d, nz)))
 
     def thin_gather(p):
-        arrived(thin_b.at[p, pl.ds(0, nb - 1)], 8 * p + 5)
-        thin_all[p, x] = total([thin_b[p, i] for i in range(nb)])
+        arrived(thin_z.at[p, pl.ds(0, nz - 1)], 8 * p + 4)
+        thin_zll[p, x] = total([thin_z[p, i] for i in range(nz)])
         for dx in along_x:
-            remote(thin_all.at[p, x], thin_all.at[p, x], 8 * p + 6, in_plane(t, turned_x(dx)))
+            remote(thin_zll.at[p, x], thin_zll.at[p, x], 8 * p + 6, in_plane(t, turned_x(dx)))
 
     def thin_result(p):
-        arrived(thin_all.at[p, pl.ds(0, nx - 1)], 8 * p + 6)
-        return jnp.concatenate([thin_all[p, j] for j in range(nx)], axis=0)
+        arrived(thin_zll.at[p, pl.ds(0, nx - 1)], 8 * p + 6)
+        return jnp.concatenate([thin_zll[p, j] for j in range(nx)], axis=0)
 
     for i in range(3):
         loads[i].wait()
     terms = split3(bo[...])
     value = fold3(rows_by_rows(terms, go[...]) + rows_by_rows(terms, eo[...]))
-    pl.semaphore_wait(barrier, len(plane) + len(along_z))
+    pl.semaphore_wait(barrier, len(plane) + 2 * reach)
+    for d in (reach, nz - reach):
+        pl.semaphore_signal(relay_sem, inc=1, device_id=at_z(lax.rem(z + d, nz)), device_id_type=MESH)
     thin_scatter(0, value)
     for i in range(3, 6):
         loads[i].wait()
     terms = split3(bq[...])
     value = fold3(rows_by_rows(terms, gq[...]) + rows_by_rows(terms, eq[...]))
     wide_scatter(0, value)
-    thin_near(0)
+    pl.semaphore_wait(relay_sem, 2)
+    thin_exchange(0)
     wide_exchange(0)
-    thin_far(0)
     thin_gather(0)
     wide_gather(0)
 
@@ -215,33 +212,31 @@
     terms = split3(left_output)
     value = fold3(rows_by_columns(terms, go[...]) + rows_by_columns(terms, eo[...]))
     wide_scatter(1, value)
+    left_query = wide_result(0)
+    terms = split3(left_query)
+    value = fold3(rows_by_columns(terms, gq[...]) + rows_by_columns(terms, eq[...]))
+    thin_scatter(1, value)
     gram = exact(left_output, left_output, ((1,), (1,)))
     gram_all[t] = jnp.concatenate([gram[i : i + 8] for i in range(0, R, 8)], axis=1)
     for dy, dc, dx in plane:
         if dx == 0:
             remote(gram_all.at[t], gram_all.at[t], 7, in_plane(turned_t(dy, dc), x))
-    left_query = wide_result(0)
-    terms = split3(left_query)
-    value = fold3(rows_by_columns(terms, gq[...]) + rows_by_columns(terms, eq[...]))
-    thin_scatter(1, value)
     query_work = augmented(exact(left_query, left_query, ((1,), (1,))))
+    query_work = eliminate(query_work, 0, 12)
     wide_exchange(1)
-    thin_near(1)
+    thin_exchange(1)
+    query_work = eliminate(query_work, 12, R)
     arrived(gram_all.at[pl.ds(0, nt - 1)], 7)
     gram = total([gram_all[i] for i in range(nt)])
     gram = jnp.concatenate([gram[:, i : i + R] for i in range(0, 4 * R, R)], axis=0)
-    output_work = augmented(gram)
-    query_work = eliminate(query_work, 0, R // 2)
-    output_work = eliminate(output_work, 0, R // 2)
-    thin_far(1)
-    query_work = eliminate(query_work, R // 2, R)
-    output_work = eliminate(output_work, R // 2, R)
+    output_work = eliminate(augmented(gram), 0, 16)
+    wide_gather(1)
+    output_work = eliminate(output_work, 16, R)
+    thin_gather(1)
     query_inverse = query_work[:, R : 2 * R]
     output_inverse = output_work[:, R : 2 * R]
     uq_out[...] = exact(query_inverse, left_query, ((1,), (0,)))
     uo_out[...] = exact(output_inverse, left_output, ((1,), (0,)))
-    wide_gather(1)
-    thin_gather(1)
     ro_out[...] = exact(output_inverse, wide_result(1), ((1,), (0,)))
     rq_out[...] = exact(query_inverse, thin_result(1), ((1,), (0,)))
 
@@ -251,9 +246,8 @@
         sent(wide_z.at[p, pl.ds(0, nz - 1)], k + 1)
         sent(wide_all.at[p, pl.ds(0, nt * nx - 1)], k + 2)
         sent(thin_in.at[p], k + 3)
-        sent(thin_a.at[p, pl.ds(0, na - 1)], k + 4)
-        sent(thin_b.at[p, pl.ds(0, nb - 1)], k + 5)
-        sent(thin_all.at[p, pl.ds(0, nx - 1)], k + 6)
+        sent(thin_z.at[p, pl.ds(0, nz - 1)], k + 4)
+        sent(thin_zll.at[p, pl.ds(0, nx - 1)], k + 6)
     sent(gram_all.at[pl.ds(0, nt - 1)], 7)
 
 
@@ -286,7 +280,7 @@
 
 
 def local(sizes, grad_query, error_query, basis_query, grad_output, error_output, basis_output):
-    ny, nc, nx, na, nb = sizes
+    ny, nc, nx, nz = sizes
     nt = ny * nc
     gq, eq, go, eo = grad_query[0], error_query[0], grad_output[0], error_output[0]
     rows, columns = gq.shape
@@ -296,7 +290,7 @@
     vmem = pl.BlockSpec(memory_space=pltpu.VMEM)
     shape = jax.ShapeDtypeStruct
     uq, rq, uo, ro = pl.pallas_call(
-        functools.partial(exchange, ny, nc, nx, na, nb),
+        functools.partial(exchange, ny, nc, nx, nz),
         out_shape=(
             shape((R, rows), F32), shape((R, columns), F32), shape((R, hidden), F32), shape((R, features), F32),
         ),
@@ -312,30 +306,47 @@
             pltpu.SemaphoreType.DMA((6,)),
             pltpu.VMEM((2, nt, nx, part, LANES), F32),
             pltpu.VMEM((2, nt * nx - 1, part, LANES), F32),
-            pltpu.VMEM((2, na * nb, part, LANES), F32),
+            pltpu.VMEM((2, nz, part, LANES), F32),
             pltpu.VMEM((2, nt * nx, part, LANES), F32),
             pltpu.VMEM((2, nx, part, hidden), F32),
             pltpu.VMEM((2, nx - 1, part, hidden), F32),
-            pltpu.VMEM((2, na, part, hidden), F32),
-            pltpu.VMEM((2, nb, part, hidden), F32),
+            pltpu.VMEM((2, nz, part, hidden), F32),
             pltpu.VMEM((2, nx, part, hidden), F32),
             pltpu.VMEM((nt, 8, LANES), F32),
             pltpu.SemaphoreType.DMA((16,)),
             pltpu.SemaphoreType.DMA((16,)),
+            pltpu.SemaphoreType.REGULAR,
         ],
         compiler_params=pltpu.CompilerParams(
             collective_id=0, has_side_effects=True, vmem_limit_bytes=60 * 1024 * 1024
         ),
     )(gq, eq, basis_query.T, go, eo, basis_output.T)
     outs = pl.pallas_call(
-        functools.partial(finish, nx * na * nb),
+        functools.partial(finish, nx * nz),
         out_shape=(
             shape((rows, columns), BF16), shape((hidden, features), BF16),
             shape((rows, columns), BF16), shape((hidden, features), BF16),
             shape((R, columns), F32), shape((R, features), F32),
         ),
-        in_specs=[vmem] * 8,
-        out_specs=(vmem,) * 6,
+        grid=(2,),
+        in_specs=[
+            pl.BlockSpec((R, rows // 2), lambda i: (0, i)),
+            pl.BlockSpec((R, columns), lambda i: (0, 0)),
+            pl.BlockSpec((R, hidden // 2), lambda i: (0, i)),
+            pl.BlockSpec((R, features), lambda i: (0, 0)),
+            pl.BlockSpec((rows // 2, columns), lambda i: (i, 0)),
+            pl.BlockSpec((rows // 2, columns), lambda i: (i, 0)),
+            pl.BlockSpec((hidden // 2, features), lambda i: (i, 0)),
+            pl.BlockSpec((hidden // 2, features), lambda i: (i, 0)),
+        ],
+        out_specs=(
+            pl.BlockSpec((rows // 2, columns), lambda i: (i, 0)),
+            pl.BlockSpec((hidden // 2, features), lambda i: (i, 0)),
+            pl.BlockSpec((rows // 2, columns), lambda i: (i, 0)),
+            pl.BlockSpec((hidden // 2, features), lambda i: (i, 0)),
+            pl.BlockSpec((R, columns), lambda i: (0, 0)),
+            pl.BlockSpec((R, features), lambda i: (0, 0)),
+        ),
         compiler_params=pltpu.CompilerParams(vmem_limit_bytes=60 * 1024 * 1024),
     )(uq, rq, uo, ro, gq, eq, go, eo)
     return outs[0], outs[1], outs[2][None], outs[3][None], outs[4].T, outs[5].T
@@ -344,10 +355,8 @@
 def solution(mesh):
     nt, n = mesh.shape["tensor"], mesh.shape["dp"]
     nx = 4 if n >= 64 else 2
-    na = 4 if n >= 64 else 2
-    nb = n // (nx * na)
     return jax.shard_map(
-        functools.partial(local, (nt // 2, 2, nx, na, nb)),
+        functools.partial(local, (nt // 2, 2, nx, n // nx)),
         mesh=mesh,
         in_specs=(
             P("dp", None, "tensor"),

time: 62.8 us -> 57.7 us (0.919)
  Pallas kernels: 62 us -> 56.9 us
    pallas_call x2, Pallas kernels: 62 us -> 56.9 us  [the longest x1 53.8 us: local(): pl.pallas_call(functools.partial(exchange, ny, nc, nx, nz), out_shape=(sh...]
where the time goes in v3:
time: 57.7 us; the launch traced here: 57.6 us
  Pallas kernels  56.9 us (99%)
  between operations  0.64 us (1%)
    pallas_call x1, Pallas kernels, local(): pl.pallas_call(functools.partial(exchange, ny, nc, nx, nz), out_shape=(sh...  53.8 us
    pallas_call x1, Pallas kernels, local(): pl.pallas_call(functools.partial(finish, nx * nz), out_shape=(shape((rows...  3.14 us

profile of v3, /device:TPU:2, one launch (start us, length us, event | category | flops | bytes accessed | tf_op | source)
XLA Modules:
  0.0 57.6 jit_solution(6867117012618726594)
XLA Ops:
  0.6 53.8 %shard_map.109 = (f32[32,1024]{1,0:T(8,128)}, f32[32,256]{1,0:T(8,128)}, f32[32,256]{1,0:T(8,128)}, f32[32,1024]{1,0:T(8,128)}) custom-call(bf16[1024,256]{1,0:T(8,128)(2,1)} %bitcast.10, bf16[1024,256]{1,0:T(8,128)(2,1)} %bitcast.12, f32[32,256]{1,0:T(8,128)} %bitcast.19, bf16[256,1024]{1,0:T(8,128)(2,1)} %bitcast.14, bf16[256,1024]{1,0:T(8,128)(2,1)} %bitcast.16, ...), custom_call_target="tpu_custom_call" | custom-call | tf_op jit(solution)/shard_map/pallas_call | solution.py:292
  54.4 3.1 %shard_map.110 = (bf16[1024,256]{1,0:T(8,128)(2,1)}, bf16[256,1024]{1,0:T(8,128)(2,1)}, bf16[1024,256]{1,0:T(8,128)(2,1)}, bf16[256,1024]{1,0:T(8,128)(2,1)}, f32[32,256]{1,0:T(8,128)}, /*index=5*/f32[32,1024]{1,0:T(8,128)}) custom-call(f32[32,1024]{1,0:T(8,128)} %get-tuple-element.16.uq, f32[32,256]{1,0:T(8,128)} %get-tuple-element.17.rq, ...), custom_call_target="tpu_custom_call" | custom-call | tf_op jit(solution)/shard_map/pallas_call | solution.py:324

commit v4 on v3

--- a/solution.py
+++ b/solution.py
@@ -40,16 +40,24 @@
     )
 
 
-def eliminate(work, first, last):
-    row = lax.broadcasted_iota(jnp.int32, work.shape, 0)
+def eliminate(works, first, last):
+    row = lax.broadcasted_iota(jnp.int32, works[0].shape, 0)
     for j in range(first, last):
-        pivot = work[j : j + 1, j : j + 1]
-        inverse = lax.rsqrt(pivot)
-        inverse = inverse * (1.5 - 0.5 * (pivot * inverse) * inverse)
-        scaled = work[j : j + 1, :] * inverse
-        column = work[:, j : j + 1] * inverse
-        work = jnp.where(row > j, work - column * scaled, jnp.where(row == j, scaled, work))
-    return work
+        columns = [jnp.broadcast_to(work[:, j : j + 1], work.shape) for work in works]
+        inverses = [1.0 / column[j : j + 1] for column in columns]
+        scaled = [work[j : j + 1] * inverse for work, inverse in zip(works, inverses)]
+        works = [
+            jnp.where(row > j, work - column * pivot_row, work)
+            for work, column, pivot_row in zip(works, columns, scaled)
+        ]
+    return works
+
+
+def lower_inverse(work):
+    rows = lax.broadcasted_iota(jnp.int32, (R, R), 0)
+    columns = lax.broadcasted_iota(jnp.int32, (R, R), 1)
+    pivots = jnp.sum(jnp.where(rows == columns, work[:, :R], 0.0), axis=1, keepdims=True)
+    return work[:, R : 2 * R] / jnp.sqrt(pivots)
 
 
 def augmented(gram):
@@ -65,7 +73,7 @@
     uq_out, rq_out, uo_out, ro_out,
     gq, eq, bq, go, eo, bo, load_sem,
     wide_here, wide_in, wide_z, wide_all,
-    thin_here, thin_in, thin_z, thin_zll,
+    thin_here, thin_in, thin_z, thin_all,
     gram_all, send_sem, recv_sem, relay_sem,
 ):
     nt = ny * nc
@@ -181,13 +189,13 @@
 
     def thin_gather(p):
         arrived(thin_z.at[p, pl.ds(0, nz - 1)], 8 * p + 4)
-        thin_zll[p, x] = total([thin_z[p, i] for i in range(nz)])
+        thin_all[p, x] = total([thin_z[p, i] for i in range(nz)])
         for dx in along_x:
-            remote(thin_zll.at[p, x], thin_zll.at[p, x], 8 * p + 6, in_plane(t, turned_x(dx)))
+            remote(thin_all.at[p, x], thin_all.at[p, x], 8 * p + 6, in_plane(t, turned_x(dx)))
 
     def thin_result(p):
-        arrived(thin_zll.at[p, pl.ds(0, nx - 1)], 8 * p + 6)
-        return jnp.concatenate([thin_zll[p, j] for j in range(nx)], axis=0)
+        arrived(thin_all.at[p, pl.ds(0, nx - 1)], 8 * p + 6)
+        return jnp.concatenate([thin_all[p, j] for j in range(nx)], axis=0)
 
     for i in range(3):
         loads[i].wait()
@@ -212,29 +220,25 @@
     terms = split3(left_output)
     value = fold3(rows_by_columns(terms, go[...]) + rows_by_columns(terms, eo[...]))
     wide_scatter(1, value)
-    left_query = wide_result(0)
-    terms = split3(left_query)
-    value = fold3(rows_by_columns(terms, gq[...]) + rows_by_columns(terms, eq[...]))
-    thin_scatter(1, value)
     gram = exact(left_output, left_output, ((1,), (1,)))
     gram_all[t] = jnp.concatenate([gram[i : i + 8] for i in range(0, R, 8)], axis=1)
     for dy, dc, dx in plane:
         if dx == 0:
             remote(gram_all.at[t], gram_all.at[t], 7, in_plane(turned_t(dy, dc), x))
-    query_work = augmented(exact(left_query, left_query, ((1,), (1,))))
-    query_work = eliminate(query_work, 0, 12)
+    left_query = wide_result(0)
+    terms = split3(left_query)
+    value = fold3(rows_by_columns(terms, gq[...]) + rows_by_columns(terms, eq[...]))
+    thin_scatter(1, value)
+    query_gram = exact(left_query, left_query, ((1,), (1,)))
     wide_exchange(1)
     thin_exchange(1)
-    query_work = eliminate(query_work, 12, R)
     arrived(gram_all.at[pl.ds(0, nt - 1)], 7)
     gram = total([gram_all[i] for i in range(nt)])
     gram = jnp.concatenate([gram[:, i : i + R] for i in range(0, 4 * R, R)], axis=0)
-    output_work = eliminate(augmented(gram), 0, 16)
+    works = eliminate([augmented(query_gram), augmented(gram)], 0, R)
+    query_inverse, output_inverse = [lower_inverse(work) for work in works]
     wide_gather(1)
-    output_work = eliminate(output_work, 16, R)
     thin_gather(1)
-    query_inverse = query_work[:, R : 2 * R]
-    output_inverse = output_work[:, R : 2 * R]
     uq_out[...] = exact(query_inverse, left_query, ((1,), (0,)))
     uo_out[...] = exact(output_inverse, left_output, ((1,), (0,)))
     ro_out[...] = exact(output_inverse, wide_result(1), ((1,), (0,)))
@@ -247,7 +251,7 @@
         sent(wide_all.at[p, pl.ds(0, nt * nx - 1)], k + 2)
         sent(thin_in.at[p], k + 3)
         sent(thin_z.at[p, pl.ds(0, nz - 1)], k + 4)
-        sent(thin_zll.at[p, pl.ds(0, nx - 1)], k + 6)
+        sent(thin_all.at[p, pl.ds(0, nx - 1)], k + 6)
     sent(gram_all.at[pl.ds(0, nt - 1)], 7)
 
 

time: 57.7 us -> 55.6 us (0.964)
  Pallas kernels: 56.9 us -> 54.8 us
    pallas_call x1, Pallas kernels: 53.8 us -> 51.7 us  [local(): pl.pallas_call(functools.partial(exchange, ny, nc, nx, nz), out_shape=(sh...]
where the time goes in v4:
time: 55.6 us; the launch traced here: 55.5 us
  Pallas kernels  54.8 us (99%)
  between operations  0.64 us (1%)
    pallas_call x1, Pallas kernels, local(): pl.pallas_call(functools.partial(exchange, ny, nc, nx, nz), out_shape=(sh...  51.7 us
    pallas_call x1, Pallas kernels, local(): pl.pallas_call(functools.partial(finish, nx * nz), out_shape=(shape((rows...  3.14 us

profile of v4, /device:TPU:2, one launch (start us, length us, event | category | flops | bytes accessed | tf_op | source)
XLA Modules:
  0.0 55.5 jit_solution(4765293482641733551)
XLA Ops:
  0.6 51.7 %shard_map.109 = (f32[32,1024]{1,0:T(8,128)}, f32[32,256]{1,0:T(8,128)}, f32[32,256]{1,0:T(8,128)}, f32[32,1024]{1,0:T(8,128)}) custom-call(bf16[1024,256]{1,0:T(8,128)(2,1)} %bitcast.10, bf16[1024,256]{1,0:T(8,128)(2,1)} %bitcast.12, f32[32,256]{1,0:T(8,128)} %bitcast.19, bf16[256,1024]{1,0:T(8,128)(2,1)} %bitcast.14, bf16[256,1024]{1,0:T(8,128)(2,1)} %bitcast.16, ...), custom_call_target="tpu_custom_call" | custom-call | tf_op jit(solution)/shard_map/pallas_call | solution.py:296
  52.3 3.1 %shard_map.110 = (bf16[1024,256]{1,0:T(8,128)(2,1)}, bf16[256,1024]{1,0:T(8,128)(2,1)}, bf16[1024,256]{1,0:T(8,128)(2,1)}, bf16[256,1024]{1,0:T(8,128)(2,1)}, f32[32,256]{1,0:T(8,128)}, /*index=5*/f32[32,1024]{1,0:T(8,128)}) custom-call(f32[32,1024]{1,0:T(8,128)} %get-tuple-element.16.uq, f32[32,256]{1,0:T(8,128)} %get-tuple-element.17.rq, ...), custom_call_target="tpu_custom_call" | custom-call | tf_op jit(solution)/shard_map/pallas_call | solution.py:328

commit v5 on v4

--- a/solution.py
+++ b/solution.py
@@ -70,8 +70,8 @@
 def exchange(
     ny, nc, nx, nz,
     gq_hbm, eq_hbm, bq_hbm, go_hbm, eo_hbm, bo_hbm,
-    uq_out, rq_out, uo_out, ro_out,
-    gq, eq, bq, go, eo, bo, load_sem,
+    uq_out, rq_out, uo_out, ro_out, gq, eq, go, eo,
+    bq, bo, load_sem,
     wide_here, wide_in, wide_z, wide_all,
     thin_here, thin_in, thin_z, thin_all,
     gram_all, send_sem, recv_sem, relay_sem,
@@ -293,19 +293,17 @@
     hbm = pl.BlockSpec(memory_space=pltpu.HBM)
     vmem = pl.BlockSpec(memory_space=pltpu.VMEM)
     shape = jax.ShapeDtypeStruct
-    uq, rq, uo, ro = pl.pallas_call(
+    uq, rq, uo, ro, gq, eq, go, eo = pl.pallas_call(
         functools.partial(exchange, ny, nc, nx, nz),
         out_shape=(
             shape((R, rows), F32), shape((R, columns), F32), shape((R, hidden), F32), shape((R, features), F32),
+            shape((rows, columns), BF16), shape((rows, columns), BF16),
+            shape((hidden, features), BF16), shape((hidden, features), BF16),
         ),
         in_specs=[hbm] * 6,
-        out_specs=(vmem,) * 4,
+        out_specs=(vmem,) * 8,
         scratch_shapes=[
-            pltpu.VMEM((rows, columns), BF16),
-            pltpu.VMEM((rows, columns), BF16),
             pltpu.VMEM((R, columns), F32),
-            pltpu.VMEM((hidden, features), BF16),
-            pltpu.VMEM((hidden, features), BF16),
             pltpu.VMEM((R, features), F32),
             pltpu.SemaphoreType.DMA((6,)),
             pltpu.VMEM((2, nt, nx, part, LANES), F32),
@@ -322,9 +320,9 @@
             pltpu.SemaphoreType.REGULAR,
         ],
         compiler_params=pltpu.CompilerParams(
-            collective_id=0, has_side_effects=True, vmem_limit_bytes=60 * 1024 * 1024
-        ),
-    )(gq, eq, basis_query.T, go, eo, basis_output.T)
+            collective_id=0, has_side_effects=True, vmem_limit_bytes=24576 * 1024
+        ),
+    )(*(pltpu.with_memory_space_constraint(i, pltpu.HBM) for i in (gq, eq, basis_query.T, go, eo, basis_output.T)))
     outs = pl.pallas_call(
         functools.partial(finish, nx * nz),
         out_shape=(
@@ -332,26 +330,9 @@
             shape((rows, columns), BF16), shape((hidden, features), BF16),
             shape((R, columns), F32), shape((R, features), F32),
         ),
-        grid=(2,),
-        in_specs=[
-            pl.BlockSpec((R, rows // 2), lambda i: (0, i)),
-            pl.BlockSpec((R, columns), lambda i: (0, 0)),
-            pl.BlockSpec((R, hidden // 2), lambda i: (0, i)),
-            pl.BlockSpec((R, features), lambda i: (0, 0)),
-            pl.BlockSpec((rows // 2, columns), lambda i: (i, 0)),
-            pl.BlockSpec((rows // 2, columns), lambda i: (i, 0)),
-            pl.BlockSpec((hidden // 2, features), lambda i: (i, 0)),
-            pl.BlockSpec((hidden // 2, features), lambda i: (i, 0)),
-        ],
-        out_specs=(
-            pl.BlockSpec((rows // 2, columns), lambda i: (i, 0)),
-            pl.BlockSpec((hidden // 2, features), lambda i: (i, 0)),
-            pl.BlockSpec((rows // 2, columns), lambda i: (i, 0)),
-            pl.BlockSpec((hidden // 2, features), lambda i: (i, 0)),
-            pl.BlockSpec((R, columns), lambda i: (0, 0)),
-            pl.BlockSpec((R, features), lambda i: (0, 0)),
-        ),
-        compiler_params=pltpu.CompilerParams(vmem_limit_bytes=60 * 1024 * 1024),
+        in_specs=[vmem] * 8,
+        out_specs=(vmem,) * 6,
+        compiler_params=pltpu.CompilerParams(vmem_limit_bytes=24 * 1024 * 1024),
     )(uq, rq, uo, ro, gq, eq, go, eo)
     return outs[0], outs[1], outs[2][None], outs[3][None], outs[4].T, outs[5].T
 

time: 55.6 us -> 53.7 us (0.966)
  Pallas kernels: 54.8 us -> 52.9 us
    pallas_call x1, Pallas kernels: 3.14 us -> 1.87 us  [local(): pl.pallas_call(functools.partial(finish, nx * nz), out_shape=(shape((rows...]
    pallas_call x1, Pallas kernels: 51.7 us -> 51 us  [local(): pl.pallas_call(functools.partial(exchange, ny, nc, nx, nz), out_shape=(sh...]
where the time goes in v5:
time: 53.7 us; the launch traced here: 53.5 us
  Pallas kernels  52.9 us (99%)
  between operations  0.64 us (1%)
    pallas_call x1, Pallas kernels, local(): pl.pallas_call(functools.partial(exchange, ny, nc, nx, nz), out_shape=(sh...  51 us
    pallas_call x1, Pallas kernels, local(): pl.pallas_call(functools.partial(finish, nx * nz), out_shape=(shape((rows...  1.87 us

profile of v5, /device:TPU:2, one launch (start us, length us, event | category | flops | bytes accessed | tf_op | source)
XLA Modules:
  0.0 53.5 jit_solution(17745350195060669221)
XLA Ops:
  0.6 51.0 %shard_map.109 = (f32[32,1024]{1,0:T(8,128)S(1)}, f32[32,256]{1,0:T(8,128)S(1)}, f32[32,256]{1,0:T(8,128)S(1)}, f32[32,1024]{1,0:T(8,128)S(1)}, bf16[1024,256]{1...) custom-call(bf16[1024,256]{1,0:T(8,128)(2,1)} %bitcast.10, ...), custom_call_target="tpu_custom_call" | custom-call | tf_op jit(solution)/shard_map/pallas_call | solution.py:296
  51.7 1.9 %shard_map.110 = (bf16[1024,256]{1,0:T(8,128)(2,1)}, bf16[256,1024]{1,0:T(8,128)(2,1)}, bf16[1024,256]{1,0:T(8,128)(2,1)}, bf16[256,1024]{1,0:T(8,128)(2,1)}, f32[32,256]{1,0:T(8,128)}, /*index=5*/f32[32,1024]{1,0:T(8,128)}) custom-call(f32[32,1024]{1,0:T(8,128)S(1)} %get-tuple-element.20.uq, f32[32,256]{1,0:T(8,128)S(1)} %get-tuple-element.21.rq, ...), custom_call_target="tpu_custom_call" | custom-call | tf_op jit(solution)/shard_map/pallas_call | solution.py:326

commit v6 on v5

--- a/solution.py
+++ b/solution.py
@@ -255,32 +255,43 @@
     sent(gram_all.at[pl.ds(0, nt - 1)], 7)
 
 
-def stacked(left, right):
-    left_high = left.astype(BF16)
-    left_low = (left - left_high.astype(F32)).astype(BF16)
-    right_high = right.astype(BF16)
-    right_low = (right - right_high.astype(F32)).astype(BF16)
-    return lax.dot_general(
-        jnp.concatenate([left_high, left_low, left_high], axis=0),
-        jnp.concatenate([right_high, right_high, right_low], axis=0),
-        (((0,), (0,)), ((), ())),
-        preferred_element_type=F32,
-    )
-
-
 def finish(
-    replicas, uq, rq, uo, ro, gq, eq, go, eo,
+    replicas, parts, uq, rq, uo, ro, gq, eq, go, eo,
     reduced_query, reduced_output, error_query, error_output, right_query, right_output,
+    rounded_query, rounded_output, next_query, next_output, sem,
 ):
+    copies = []
+
+    def store(source, target):
+        copy = pltpu.make_async_copy(source, target, sem.at[len(copies)])
+        copy.start()
+        copies.append(copy)
+
+    store(ro, right_output)
+    store(rq, right_query)
     scale = 1.0 / replicas
-    approx = stacked(uq[...], rq[...])
-    reduced_query[...] = approx.astype(BF16)
-    error_query[...] = (gq[...].astype(F32) + eq[...].astype(F32) - approx * scale).astype(BF16)
-    approx = stacked(uo[...], ro[...])
-    reduced_output[...] = approx.astype(BF16)
-    error_output[...] = (go[...].astype(F32) + eo[...].astype(F32) - approx * scale).astype(BF16)
-    right_query[...] = rq[...]
-    right_output[...] = ro[...]
+    for u, r, g, e, rounded, following, reduced, error in (
+        (uq, rq, gq, eq, rounded_query, next_query, reduced_query, error_query),
+        (uo, ro, go, eo, rounded_output, next_output, reduced_output, error_output),
+    ):
+        left, right = u[...], r[...]
+        left_high, right_high = left.astype(BF16), right.astype(BF16)
+        left_low = (left - left_high.astype(F32)).astype(BF16)
+        right_low = (right - right_high.astype(F32)).astype(BF16)
+        left = jnp.concatenate([left_high, left_low, left_high], axis=0)
+        right = jnp.concatenate([right_high, right_high, right_low], axis=0)
+        rows = g.shape[0] // parts
+        for i in range(parts):
+            at = pl.ds(i * rows, rows)
+            approx = lax.dot_general(
+                left[:, i * rows : (i + 1) * rows], right, (((0,), (0,)), ((), ())), preferred_element_type=F32
+            )
+            rounded[at] = approx.astype(BF16)
+            following[at] = (g[at].astype(F32) + e[at].astype(F32) - approx * scale).astype(BF16)
+            store(rounded.at[at], reduced.at[at])
+            store(following.at[at], error.at[at])
+    for copy in copies:
+        copy.wait()
 
 
 def local(sizes, grad_query, error_query, basis_query, grad_output, error_output, basis_output):
@@ -290,6 +301,7 @@
     rows, columns = gq.shape
     hidden, features = go.shape
     part = R // nx
+    parts = 4
     hbm = pl.BlockSpec(memory_space=pltpu.HBM)
     vmem = pl.BlockSpec(memory_space=pltpu.VMEM)
     shape = jax.ShapeDtypeStruct
@@ -324,14 +336,21 @@
         ),
     )(*(pltpu.with_memory_space_constraint(i, pltpu.HBM) for i in (gq, eq, basis_query.T, go, eo, basis_output.T)))
     outs = pl.pallas_call(
-        functools.partial(finish, nx * nz),
+        functools.partial(finish, nx * nz, parts),
         out_shape=(
             shape((rows, columns), BF16), shape((hidden, features), BF16),
             shape((rows, columns), BF16), shape((hidden, features), BF16),
             shape((R, columns), F32), shape((R, features), F32),
         ),
         in_specs=[vmem] * 8,
-        out_specs=(vmem,) * 6,
+        out_specs=(hbm,) * 6,
+        scratch_shapes=[
+            pltpu.VMEM((rows, columns), BF16),
+            pltpu.VMEM((hidden, features), BF16),
+            pltpu.VMEM((rows, columns), BF16),
+            pltpu.VMEM((hidden, features), BF16),
+            pltpu.SemaphoreType.DMA((2 + 4 * parts,)),
+        ],
         compiler_params=pltpu.CompilerParams(vmem_limit_bytes=24 * 1024 * 1024),
     )(uq, rq, uo, ro, gq, eq, go, eo)
     return outs[0], outs[1], outs[2][None], outs[3][None], outs[4].T, outs[5].T

time: 53.7 us -> 53.5 us (level)
  no operation moved by 1% of the time
where the time goes in v6:
time: 53.5 us; the launch traced here: 53.4 us
  Pallas kernels  52.8 us (99%)
  between operations  0.64 us (1%)
    pallas_call x1, Pallas kernels, local(): pl.pallas_call(functools.partial(exchange, ny, nc, nx, nz), out_shape=(sh...  51 us
    pallas_call x1, Pallas kernels, local(): pl.pallas_call(functools.partial(finish, nx * nz, parts), out_shape=(shap...  1.73 us

profile of v6, /device:TPU:2, one launch (start us, length us, event | category | flops | bytes accessed | tf_op | source)
XLA Modules:
  0.0 53.4 jit_solution(16400269846269511418)
XLA Ops:
  0.6 51.0 %shard_map.109 = (f32[32,1024]{1,0:T(8,128)S(1)}, f32[32,256]{1,0:T(8,128)S(1)}, f32[32,256]{1,0:T(8,128)S(1)}, f32[32,1024]{1,0:T(8,128)S(1)}, bf16[1024,256]{1...) custom-call(bf16[1024,256]{1,0:T(8,128)(2,1)} %bitcast.10, ...), custom_call_target="tpu_custom_call" | custom-call | tf_op jit(solution)/shard_map/pallas_call | solution.py:308
  51.7 1.7 %shard_map.110 = (bf16[1024,256]{1,0:T(8,128)(2,1)}, bf16[256,1024]{1,0:T(8,128)(2,1)}, bf16[1024,256]{1,0:T(8,128)(2,1)}, bf16[256,1024]{1,0:T(8,128)(2,1)}, f32[32,256]{1,0:T(8,128)}, /*index=5*/f32[32,1024]{1,0:T(8,128)}) custom-call(f32[32,1024]{1,0:T(8,128)S(1)} %get-tuple-element.20.uq, f32[32,256]{1,0:T(8,128)S(1)} %get-tuple-element.21.rq, ...), custom_call_target="tpu_custom_call" | custom-call | tf_op jit(solution)/shard_map/pallas_call | solution.py:338
